TPU v7x, 32 devices: a whole 2x2x4 slice. The times are simulated.
32 devices in a mesh: grp: 2 (over y), sec: 4 (over z), term: 4 (over x, core).
Axes of the slice: x: 2, y: 2, z: 4, core: 2. Of those that a mesh axis runs over, the one named last changes fastest.
Arguments:
- wave_blocks: bfloat16 [16, 16, 128, 128], P(('grp', 'sec')), parts along dimension 0, may hold values from -6 to 6
- right_env: bfloat16 [48, 8, 128, 128], P(('grp', 'term'), 'sec'), parts along dimension 0, may hold values from -0.5 to 0.5
- left_env: bfloat16 [48, 8, 128, 128], P(('grp', 'term'), 'sec'), parts along dimension 0, may hold values from -0.5 to 0.5
- site_coeff: float32 [48, 16], P(('grp', 'term')), parts along dimension 0, may hold values from -0.4 to 0.4
- dest_owner: int32 [16, 16, 1], P('grp'), parts along dimension 0, may hold values from 0 to 3; in each aligned block of 32 rows (0 to 31, 32 to 63, ..., all dimensions but the last counted through in order) at most 16 rows name the same one
- sub_sector: int32 [16, 16], P('grp'), parts along dimension 0, may hold values from 0 to 1
Outputs:
- sigma: bfloat16 [16, 16, 128, 128], P(('grp', 'sec'), None, 'term'), parts along dimension 0
There are 2 independent parts, one for each index of `grp`. A program takes and returns all parts, laid end to end along the dimension named above; each array names one. Nothing has to cross between parts.
Inputs may be any that keep to these rules, and one draw needn't show every extreme that they name: `dest_owner`: among the 32 blocks of one device (right sectors in order), no owner is named more than 16 times, a bound that some block reaches.
All inputs are finite; a program needn't handle non-finite values.
Results may differ from a plain program's by a relative error of at most 0.0049.
Values may be sent and summed in bfloat16 or wider, within the bound.
A program may use at most 128 MiB of HBM per device.

v0:
```python
import jax
import jax.numpy as jnp
from jax import lax
from jax.sharding import PartitionSpec as P


def local_wave(wave_blocks, right_env, site_coeff, per_dev, side):
    product = jnp.einsum(
        "rsab,trbc->rstac", wave_blocks, right_env, preferred_element_type=jnp.float32
    )
    scaled = product * jnp.transpose(site_coeff)[None, :, :, None, None]
    return scaled.astype(jnp.bfloat16).reshape(per_dev, site_coeff.shape[0], side, side)


def local(wave_blocks, right_env, left_env, site_coeff, dest_owner, sub_sector):
    here = lax.axis_index("sec")
    sec_dev = wave_blocks.shape[0]
    phys = wave_blocks.shape[1]
    side = wave_blocks.shape[2]
    per_dev = sec_dev * phys
    wave = local_wave(wave_blocks, right_env, site_coeff, per_dev, side)
    all_left = dest_owner[:, :, 0] * sec_dev + sub_sector
    own_left = lax.dynamic_slice_in_dim(all_left, here * sec_dev, sec_dev, 0).reshape(per_dev)
    gathered = lax.all_gather(left_env, "sec", axis=1, tiled=True)
    chosen_left = jnp.take(gathered, own_left, axis=1)
    summed = jnp.einsum("tqab,qtbc->qac", chosen_left, wave, preferred_element_type=jnp.float32)
    local_part = summed.reshape(sec_dev, phys, side, side)
    result = lax.psum_scatter(local_part, "term", scatter_dimension=2, tiled=True)
    return result.astype(jnp.bfloat16)


def solution(mesh):
    placed = (
        P(("grp", "sec"), None, None, None),
        P(("grp", "term"), "sec", None, None),
        P(("grp", "term"), "sec", None, None),
        P(("grp", "term"), None),
        P("grp", None, None),
        P("grp", None),
    )
    return jax.shard_map(
        local,
        mesh=mesh,
        in_specs=placed,
        out_specs=P(("grp", "sec"), None, "term", None),
        check_vma=False,
    )
```

profile of v0, /device:TPU:0, one launch (start us, length us, event | category | flops | bytes accessed | tf_op | source)
XLA Modules:
  0.0 101.1 jit_solution(15077105799532994873)
XLA Ops:
  6.5 0.0 copy-start
  6.5 0.0 all-gather.2.cloned.1.call-start
  6.5 0.7 all-gather.2.cloned.1.call-update
  7.3 0.0 reduce-scatter.2.cloned.1.call-start
  7.3 0.7 bitcast_add_fusion
  8.0 0.1 reshape.49
  8.1 0.1 reshape.48
  8.2 0.0 copy-done
  8.2 5.9 %fusion = bf16[2,16,6,128,128]{3,4,1,2,0:T(8,128)(2,1)} fusion(f32[16,6]{0,1:T(8,128)} %bitcast.30, bf16[2,16,128,128]{3,2,1,0:T(8,128)(2,1)S(1)} %copy-done, bf16[6,2,128,128]{3,2,1,0:T(8,128)(2,1)} %param.7), kind=kOutput, calls=%fused_computation.2 | convolution fusion | flops 811597824 | bytes 7733632 | tf_op jit(solution)/shard_map/rsab,trbc->rstac/dot_general | solution.py:8
  14.1 8.7 %copy.11 = bf16[2,16,6,128,128]{4,3,2,1,0:T(8,128)(2,1)} copy(bf16[2,16,6,128,128]{3,4,1,2,0:T(8,128)(2,1)} %fusion) | data formatting | bytes 12582912 | tf_op jit(solution)/shard_map/convert_element_type | solution.py:12
  22.8 25.9 %all-gather.2.cloned.1.call-done = bf16[6,8,128,128]{3,2,1,0:T(8,128)(2,1)} async-done(((bf16[6,2,128,128]{3,2,1,0:T(8,128)(2,1)}), bf16[6,8,128,128]{3,2,1,0:T(8,128)(2,1)}) %all-gather.2.cloned.1.call-update) | async-done | bytes 1572880 | tf_op jit(solution)/shard_map/all_gather | solution.py:24
  48.8 5.4 %gather_fusion = bf16[32,6,128,128]{3,2,1,0:T(8,128)(2,1)} fusion(bf16[6,8,128,128]{3,2,1,0:T(8,128)(2,1)} %all-gather.2.cloned.1.call-done, s32[1024]{0:T(1024)S(1)} %pad_clamp_fusion), kind=kCustom, calls=%fused_computation | custom fusion | bytes 12583040 | tf_op jit(solution)/shard_map/jit(_take)/gather | solution.py:25
  54.2 7.8 %fusion.1 = f32[32,128,128,1]{2,1,3,0:T(8,128)} fusion(bf16[32,6,128,128]{3,2,1,0:T(8,128)(2,1)} %bitcast.28, bf16[32,6,128,128]{3,2,1,0:T(8,128)(2,1)} %gather_fusion, pred[32]{0:T(512)(128)(4,1)S(1)} %compare_and_fusion), kind=kOutput, calls=%fused_computation.3 | convolution fusion | flops 808452096 | bytes 14680096 | tf_op jit(solution)/shard_map/tqab,qtbc->qac/dot_general | solution.py:26
  62.0 0.0 reduce-scatter.2.cloned.1.call-update
  62.0 30.5 %reduce-scatter.2.cloned.1.call-done = f32[2,16,32,128]{3,2,1,0:T(8,128)} async-done(((f32[2,16,128,128]{3,2,1,0:T(8,128)}), f32[2,16,32,128]{3,2,1,0:T(8,128)}) %reduce-scatter.2.cloned.1.call-update) | async-done | bytes 524304 | tf_op jit(solution)/shard_map/reduce_scatter | solution.py:28
  92.4 1.8 %convert_element_type.7 = bf16[2,16,32,128]{3,2,1,0:T(8,128)(2,1)} convert(f32[2,16,32,128]{3,2,1,0:T(8,128)} %reduce-scatter.2.cloned.1.call-done) | non-fusion elementwise | flops 131072 | bytes 786432 | tf_op jit(solution)/shard_map/convert_element_type | solution.py:29
  (4 shorter events, 0.0 us)
Async XLA Ops:
  6.5 1.7 %copy-start = (bf16[2,16,128,128]{3,2,1,0:T(8,128)(2,1)S(1)}, bf16[2,16,128,128]{3,2,1,0:T(8,128)(2,1)}, u32[]{:S(2)}) copy-start(bf16[2,16,128,128]{3,2,1,0:T(8,128)(2,1)} %param.6) | copy-start | bytes 3145732
  6.5 42.2 %all-gather.2.cloned.1.call-start = ((), (), s32[]{:S(2)}) async-start(), calls=%async_computation.1 | async-start | bytes 1966080 | tf_op jit(solution)/shard_map/all_gather | solution.py:24
  7.3 85.2 %reduce-scatter.2.cloned.1.call-start = ((), (), s32[]{:S(2)}) async-start(), calls=%async_computation.2 | async-start | bytes 2621440 | tf_op jit(solution)/shard_map/reduce_scatter | solution.py:28
Sparse Core Ops, SparseCore 0:
  8.9 39.7 all-gather.1
  62.1 30.2 reduce-scatter.1
where the time goes:
time: 101 us
  waiting for transfers between devices  57.1 us (57%)
  local copies, waits for them, and re-layouts  14.3 us (14%)
  matrix products  13.7 us (14%)
  between operations  13.4 us (13%)
  other arithmetic  2.51 us (2%)
    reduce_scatter x1, waiting for transfers between devices, local(): lax.psum_scatter(local_part, 'term', scatter_dimension=2, tiled=True)  30.5 us
    all_gather x1, waiting for transfers between devices, local(): gathered = lax.all_gather(left_env, 'sec', axis=1, tiled=True)  25.9 us
    convert_element_type x1, local copies, waits for them, and re-layouts, local_wave(): scaled.astype(jnp.bfloat16)  8.67 us
    dot_general x1, matrix products, local(): jnp.einsum('tqab,qtbc->qac', chosen_left, wave, preferred_element_type=jn...  7.8 us
    dot_general x1, matrix products, local_wave(): jnp.einsum('rsab,trbc->rstac', wave_blocks, right_env, preferred_element_...  5.92 us
    gather x1, local copies, waits for them, and re-layouts, local(): chosen_left = jnp.take(gathered, own_left, axis=1)  5.41 us
  transfers between devices with their start and end apart: 2, of which 2 were waited for; matrix products, arithmetic and copies ran while one was open for 15% of the time, Pallas kernels for 0%

commit v1 on v0

v1 whole, which is shorter than its diff:
```python
import functools

import jax
import jax.numpy as jnp
from jax import lax
from jax.experimental import pallas as pl
from jax.experimental.pallas import tpu as pltpu
from jax.sharding import PartitionSpec as P

MESH = pl.DeviceIdType.MESH
GROUPS = 4


def body(
    n, nt, tc, sd, phys, side, nterm,
    wb_hbm, r_hbm, l_hbm, coeff, owner_ref, sub_ref, out_ref,
    wb, rcat, acc, s1, r1, s2, r2, *rest,
):
    nch = nt // tc
    gath, wave = rest[:nch], rest[nch:2 * nch]
    load_sem, lsem, rl_sem, send_r, send_l, recv, ssem1, rsem1, ssem2, rsem2 = rest[2 * nch:]
    g, i, t = lax.axis_index("grp"), lax.axis_index("sec"), lax.axis_index("term")
    q_all = sd * phys
    qg = q_all // GROUPS
    rows = side // nterm
    half = nterm // 2
    low = lax.rem(t, 2)
    high = t // 2
    pair = t + 1 - 2 * low
    across = lax.rem(t + half, nterm)
    has_r, has_l = i < n - 1, i > 0
    right, left = (g, jnp.minimum(i + 1, n - 1), t), (g, jnp.maximum(i - 1, 0), t)

    wb_load = pltpu.make_async_copy(wb_hbm, wb, load_sem)
    wb_load.start()
    r_loads = []
    for k in range(nt):
        for r in range(sd):
            cp = pltpu.make_async_copy(
                r_hbm.at[k, r], rcat.at[r, k // tc, :, pl.ds((k % tc) * side, side)], rl_sem.at[k, r]
            )
            cp.start()
            r_loads.append(cp)
    own_loads = []
    for c in range(nch):
        cp = pltpu.make_async_copy(l_hbm.at[pl.ds(c * tc, tc)], gath[c].at[i], lsem.at[c])
        cp.start()
        own_loads.append(cp)

    barrier = pltpu.get_barrier_semaphore()

    @pl.when(has_r)
    def _():
        pl.semaphore_signal(barrier, inc=1, device_id=right, device_id_type=MESH)

    @pl.when(has_l)
    def _():
        pl.semaphore_signal(barrier, inc=1, device_id=left, device_id_type=MESH)

    for peer in (pair, across):
        pl.semaphore_signal(barrier, inc=1, device_id=(g, i, peer), device_id_type=MESH)
    pl.semaphore_wait(barrier, 2 + has_r.astype(jnp.int32) + has_l.astype(jnp.int32))

    def piece(c, origin, to_right, own):
        dst = gath[c].at[origin]
        src = l_hbm.at[pl.ds(c * tc, tc)] if own else dst
        return pltpu.make_async_remote_copy(
            src_ref=src, dst_ref=dst,
            send_sem=(send_r if to_right else send_l).at[c, origin],
            recv_sem=recv.at[c, origin],
            device_id=right if to_right else left, device_id_type=MESH,
        )

    for c in range(nch):
        @pl.when(has_r)
        def _(c=c):
            piece(c, i, True, True).start()

        @pl.when(has_l)
        def _(c=c):
            piece(c, i, False, True).start()

    def relay(s, c):
        from_l, from_r = i - 1 - s, i + 1 + s

        @pl.when(from_l >= 0)
        def _():
            piece(c, from_l, True, False).wait_recv()

            @pl.when(has_r)
            def _():
                piece(c, from_l, True, False).start()

        @pl.when(from_r <= n - 1)
        def _():
            piece(c, from_r, False, False).wait_recv()

            @pl.when(has_l)
            def _():
                piece(c, from_r, False, False).start()

    wb_load.wait()
    for cp in r_loads:
        cp.wait()

    def wave_part(r, lo, hi):
        def step(k, _):
            for c in range(nch):
                s0 = 2 * k
                lhs = wb[r, pl.ds(s0, 2)].reshape(2 * side, side)
                prod = jnp.dot(lhs, rcat[r, c], preferred_element_type=jnp.float32)
                for j in range(2):
                    for u in range(tc):
                        scaled = prod[j * side:(j + 1) * side, u * side:(u + 1) * side] * coeff[c * tc + u, s0 + j]
                        wave[c][r * phys + s0 + j, u * side:(u + 1) * side, :] = scaled.astype(jnp.bfloat16)
            return 0

        lax.fori_loop(lo, hi, step, 0)

    def product(c, q):
        r, s = q // phys, lax.rem(q, phys)
        own, sub = owner_ref[i * sd + r, s], sub_ref[i * sd + r, s]
        lhs = jnp.concatenate([gath[c][own, u, sub] for u in range(tc)], axis=1)
        return jnp.dot(lhs, wave[c][q], preferred_element_type=jnp.float32)

    pairs = phys // 2
    wave_part(0, 0, pairs)
    wave_part(1, 0, pairs // 2)
    for r in range(2, sd):
        wave_part(r, 0, pairs)
    if n > 2:
        relay(0, 0)
    wave_part(1, pairs // 2, pairs)
    if n > 2:
        for c in range(1, nch):
            relay(0, c)
        def steps(s, _):
            for c in range(nch):
                relay(s, c)
            return 0
        lax.fori_loop(1, n - 2, steps, 0)
    for cp in own_loads:
        cp.wait()

    for c in range(nch - 1):
        relay(n - 2, c)

        def add(q, _, c=c):
            p = product(c, q)
            acc[q] = p if c == 0 else acc[q] + p
            return 0

        lax.fori_loop(0, q_all, add, 0, unroll=2)
    last = nch - 1
    relay(n - 2, last)

    def hop1(k):
        return pltpu.make_async_remote_copy(
            src_ref=s1.at[k], dst_ref=r1.at[k], send_sem=ssem1.at[k], recv_sem=rsem1.at[k],
            device_id=(g, i, pair), device_id_type=MESH,
        )

    def hop2(k):
        return pltpu.make_async_remote_copy(
            src_ref=s2.at[k], dst_ref=r2.at[k], send_sem=ssem2.at[k], recv_sem=rsem2.at[k],
            device_id=(g, i, across), device_id_type=MESH,
        )

    def rows_of(dest):
        return pl.ds(pl.multiple_of(dest * rows, rows), rows)

    def middle(k):
        hop1(k).wait_recv()

        def one(j, _):
            q = k * qg + j
            away = acc[q, rows_of((1 - high) * 2 + low)] + r1[k, j, 1 - high].astype(jnp.float32)
            s2[k, j] = away.astype(jnp.bfloat16)
            return 0

        lax.fori_loop(0, qg, one, 0, unroll=4)
        hop2(k).start()

    for k in range(GROUPS):
        def finish(j, _, k=k):
            q = k * qg + j
            acc[q] = acc[q] + product(last, q)
            for h in range(half):
                s1[k, j, h] = acc[q, rows_of(2 * h + 1 - low)].astype(jnp.bfloat16)
            return 0

        lax.fori_loop(0, qg, finish, 0, unroll=2)
        hop1(k).start()
        if k >= 1:
            middle(k - 1)
    middle(GROUPS - 1)
    for k in range(GROUPS):
        hop2(k).wait_recv()

        def close(j, _, k=k):
            q = k * qg + j
            mine = acc[q, rows_of(t)] + r1[k, j, high].astype(jnp.float32)
            total = mine + r2[k, j].astype(jnp.float32)
            out_ref[q // phys, lax.rem(q, phys)] = total.astype(jnp.bfloat16)
            return 0

        lax.fori_loop(0, qg, close, 0, unroll=4)

    for k in range(GROUPS):
        hop1(k).wait_send()
        hop2(k).wait_send()

    def drain(o, _):
        for c in range(nch):
            @pl.when(jnp.logical_and(has_r, o <= i))
            def _(c=c):
                piece(c, o, True, False).wait_send()

            @pl.when(jnp.logical_and(has_l, o >= i))
            def _(c=c):
                piece(c, o, False, False).wait_send()
        return 0

    lax.fori_loop(0, n, drain, 0)


def local(n, nterm, wave_blocks, right_env, left_env, site_coeff, dest_owner, sub_sector):
    sd, phys, side, _ = wave_blocks.shape
    nt = right_env.shape[0]
    tc = 2 if nt % 2 == 0 else 1
    nch = nt // tc
    rows, half, qg = side // nterm, nterm // 2, sd * phys // GROUPS
    bf, dma = jnp.bfloat16, pltpu.SemaphoreType.DMA
    anywhere, smem = pl.BlockSpec(memory_space=pl.ANY), pl.BlockSpec(memory_space=pltpu.SMEM)
    flops = 4 * nt * sd * phys * side ** 3
    return pl.pallas_call(
        functools.partial(body, n, nt, tc, sd, phys, side, nterm),
        out_shape=jax.ShapeDtypeStruct((sd, phys, rows, side), bf),
        in_specs=[anywhere] * 3 + [smem] * 3,
        out_specs=pl.BlockSpec(memory_space=pltpu.VMEM),
        scratch_shapes=[
            pltpu.VMEM((sd, phys, side, side), bf),
            pltpu.VMEM((sd, nch, side, tc * side), bf),
            pltpu.VMEM((sd * phys, side, side), jnp.float32),
            pltpu.VMEM((GROUPS, qg, half, rows, side), bf),
            pltpu.VMEM((GROUPS, qg, half, rows, side), bf),
            pltpu.VMEM((GROUPS, qg, rows, side), bf),
            pltpu.VMEM((GROUPS, qg, rows, side), bf),
        ]
        + [pltpu.VMEM((n, tc, sd, side, side), bf)] * nch
        + [pltpu.VMEM((sd * phys, tc * side, side), bf)] * nch
        + [dma, dma((nch,)), dma((nt, sd)), dma((nch, n)), dma((nch, n)), dma((nch, n))]
        + [dma((GROUPS,))] * 4,
        compiler_params=pltpu.CompilerParams(
            collective_id=0, has_side_effects=True, vmem_limit_bytes=52 << 20
        ),
        cost_estimate=pl.CostEstimate(flops=flops, bytes_accessed=4 << 20, transcendentals=0),
        name="sigma",
    )(wave_blocks, right_env, left_env, site_coeff, dest_owner.reshape(sub_sector.shape), sub_sector)


def solution(mesh):
    placed = (
        P(("grp", "sec"), None, None, None),
        P(("grp", "term"), "sec", None, None),
        P(("grp", "term"), "sec", None, None),
        P(("grp", "term"), None),
        P("grp", None, None),
        P("grp", None),
    )
    return jax.shard_map(
        functools.partial(local, mesh.shape["sec"], mesh.shape["term"]),
        mesh=mesh,
        in_specs=placed,
        out_specs=P(("grp", "sec"), None, "term", None),
        check_vma=False,
    )
```

time: 101 us -> 48.7 us (0.48)
  waiting for transfers between devices: 57.1 us -> 0 us
  Pallas kernels: 0 us -> 43.7 us
  matrix products: 13.7 us -> 0 us
  between operations: 13.4 us -> 0.01 us
  local copies, waits for them, and re-layouts: 14.3 us -> 4.75 us
  other arithmetic: 2.51 us -> 0 us
    pallas_call x0 -> x1, Pallas kernels: none -> 43.7 us  [local(): pl.pallas_call(functools.partial(body, n, nt, tc, sd, phys, side, nterm),...]
    reduce_scatter x1 -> x0, waiting for transfers between devices: 30.5 us -> none  [local(): lax.psum_scatter(local_part, 'term', scatter_dimension=2, tiled=True)]
    all_gather x1 -> x0, waiting for transfers between devices: 25.9 us -> none  [local(): gathered = lax.all_gather(left_env, 'sec', axis=1, tiled=True)]
    dot_general x2 -> x0, matrix products: 13.7 us -> none  [the longest x1 7.8 us: local(): jnp.einsum('tqab,qtbc->qac', chosen_left, wave, preferred_element_type=jn...]
    convert_element_type x1 -> x0, local copies, waits for them, and re-layouts: 8.67 us -> none  [local_wave(): scaled.astype(jnp.bfloat16)]
    gather x1 -> x0, local copies, waits for them, and re-layouts: 5.41 us -> none  [local(): chosen_left = jnp.take(gathered, own_left, axis=1)]
    unnamed x2 -> x11, local copies, waits for them, and re-layouts: 0.01 us -> 4.75 us
    convert_element_type x1 -> x0, other arithmetic: 1.78 us -> none  [local(): return result.astype(jnp.bfloat16)]
  transfers between devices with their start and end apart: 2 -> 0, of which waited for: 2 -> 0; matrix products, arithmetic and copies ran while one was open for 15% -> 0% of each run, Pallas kernels for 0% -> 0%
where the time goes in v1:
time: 48.7 us; the launch traced here: 48.4 us
  Pallas kernels  43.7 us (90%)
  local copies, waits for them, and re-layouts  4.75 us (10%)
    pallas_call x1, Pallas kernels, local(): pl.pallas_call(functools.partial(body, n, nt, tc, sd, phys, side, nterm),...  43.7 us
    unnamed x11, local copies, waits for them, and re-layouts  4.75 us

profile of v1, /device:TPU:0, one launch (start us, length us, event | category | flops | bytes accessed | tf_op | source)
XLA Modules:
  0.0 48.4 jit_solution(17746341549031778241)
XLA Ops:
  0.0 0.0 copy-start
  0.0 1.0 %copy-done = bf16[6,2,128,128]{3,2,1,0:T(8,128)(2,1)S(1)} copy-done((bf16[6,2,128,128]{3,2,1,0:T(8,128)(2,1)S(1)}, bf16[6,2,128,128]{3,2,1,0:T(8,128)(2,1)}, u32[]{:S(2)}) %copy-start) | copy-done | bytes 393240
  1.0 0.0 copy-start.1
  1.0 1.0 %copy-done.1 = bf16[6,2,128,128]{3,2,1,0:T(8,128)(2,1)S(1)} copy-done((bf16[6,2,128,128]{3,2,1,0:T(8,128)(2,1)S(1)}, bf16[6,2,128,128]{3,2,1,0:T(8,128)(2,1)}, u32[]{:S(2)}) %copy-start.1) | copy-done | bytes 393240
  2.0 0.0 copy-start.2
  2.0 0.7 %copy-done.2 = f32[6,16]{1,0:T(8,128)S(1)} copy-done((f32[6,16]{1,0:T(8,128)S(1)}, f32[6,16]{1,0:T(8,128)}, u32[]{:S(2)}) %copy-start.2) | copy-done | bytes 408
  2.7 0.0 copy-start.3
  2.7 0.7 %copy-done.3 = s32[8,16,1]{1,2,0:T(1,128)S(1)} copy-done((s32[8,16,1]{1,2,0:T(1,128)S(1)}, s32[8,16,1]{1,2,0:T(1,128)}, u32[]{:S(2)}) %copy-start.3) | copy-done | bytes 536
  3.4 0.0 copy-start.4
  3.4 0.7 %copy-done.4 = s32[8,16]{1,0:T(8,128)S(1)} copy-done((s32[8,16]{1,0:T(8,128)S(1)}, s32[8,16]{1,0:T(8,128)}, u32[]{:S(2)}) %copy-start.4) | copy-done | bytes 536
  4.1 43.7 %sigma.1 = bf16[2,16,32,128]{3,2,1,0:T(8,128)(2,1)S(1)} custom-call(bf16[2,16,128,128]{3,2,1,0:T(8,128)(2,1)} %wb_hbm.1, bf16[6,2,128,128]{3,2,1,0:T(8,128)(2,1)S(1)} %copy-done, bf16[6,2,128,128]{3,2,1,0:T(8,128)(2,1)S(1)} %copy-done.1, f32[6,16]{1,0:T(8,128)S(1)} %copy-done.2, s32[8,16]{1,0:T(8,128)S(1)} %bitcast.1, s32[8,16]{1,0:T(8,128)S(1)} %copy-done.4), custom_call_target="tpu_custom_call" | custom-call | flops 1610612736 | bytes 4194304 | tf_op jit(solution)/shard_map/sigma/pallas_call | solution.py:236
  47.7 0.7 %copy.8 = bf16[2,16,32,128]{3,2,1,0:T(8,128)(2,1)} copy(bf16[2,16,32,128]{3,2,1,0:T(8,128)(2,1)S(1)} %sigma.1) | data formatting | bytes 524288
Async XLA Ops:
  0.0 1.0 %copy-start = (bf16[6,2,128,128]{3,2,1,0:T(8,128)(2,1)S(1)}, bf16[6,2,128,128]{3,2,1,0:T(8,128)(2,1)}, u32[]{:S(2)}) copy-start(bf16[6,2,128,128]{3,2,1,0:T(8,128)(2,1)} %r_hbm.1) | copy-start | bytes 1179652
  1.0 1.0 %copy-start.1 = (bf16[6,2,128,128]{3,2,1,0:T(8,128)(2,1)S(1)}, bf16[6,2,128,128]{3,2,1,0:T(8,128)(2,1)}, u32[]{:S(2)}) copy-start(bf16[6,2,128,128]{3,2,1,0:T(8,128)(2,1)} %l_hbm.1) | copy-start | bytes 1179652
  2.0 0.7 %copy-start.2 = (f32[6,16]{1,0:T(8,128)S(1)}, f32[6,16]{1,0:T(8,128)}, u32[]{:S(2)}) copy-start(f32[6,16]{1,0:T(8,128)} %coeff.1) | copy-start | bytes 1156
  2.7 0.7 %copy-start.3 = (s32[8,16,1]{1,2,0:T(1,128)S(1)}, s32[8,16,1]{1,2,0:T(1,128)}, u32[]{:S(2)}) copy-start(s32[8,16,1]{1,2,0:T(1,128)} %param.10) | copy-start | bytes 1540
  3.4 0.7 %copy-start.4 = (s32[8,16]{1,0:T(8,128)S(1)}, s32[8,16]{1,0:T(8,128)}, u32[]{:S(2)}) copy-start(s32[8,16]{1,0:T(8,128)} %sub_ref.1) | copy-start | bytes 1540

commit v2 on v1

--- a/solution.py
+++ b/solution.py
@@ -13,12 +13,14 @@
 
 def body(
     n, nt, tc, sd, phys, side, nterm,
-    wb_hbm, r_hbm, l_hbm, coeff, owner_ref, sub_ref, out_ref,
-    wb, rcat, acc, s1, r1, s2, r2, *rest,
+    wb_hbm, r_hbm, l_hbm, coeff_hbm, owner_hbm, sub_hbm, out_ref,
+    coeff, owner_ref, sub_ref, coeff_x, coeff_v, small_sem, wb, rcat, rcat_x, acc, bacc, s1, r1, s2, r2, s3, r3, *rest,
 ):
     nch = nt // tc
     gath, wave = rest[:nch], rest[nch:2 * nch]
-    load_sem, lsem, rl_sem, send_r, send_l, recv, ssem1, rsem1, ssem2, rsem2 = rest[2 * nch:]
+    load_sem, lsem, rl_sem, send_r, send_l, recv, ssem1, rsem1, ssem2, rsem2, ssem3, rsem3, xs, xr = rest[2 * nch:]
+    last = nch - 1
+    hr = side // 2
     g, i, t = lax.axis_index("grp"), lax.axis_index("sec"), lax.axis_index("term")
     q_all = sd * phys
     qg = q_all // GROUPS
@@ -33,6 +35,12 @@
 
     wb_load = pltpu.make_async_copy(wb_hbm, wb, load_sem)
     wb_load.start()
+    small_loads = [
+        pltpu.make_async_copy(src, dst, small_sem.at[k])
+        for k, (src, dst) in enumerate(((coeff_hbm, coeff), (owner_hbm, owner_ref), (sub_hbm, sub_ref)))
+    ]
+    for cp in small_loads:
+        cp.start()
     r_loads = []
     for k in range(nt):
         for r in range(sd):
@@ -43,7 +51,13 @@
             r_loads.append(cp)
     own_loads = []
     for c in range(nch):
-        cp = pltpu.make_async_copy(l_hbm.at[pl.ds(c * tc, tc)], gath[c].at[i], lsem.at[c])
+        if c == last:
+            my_rows = pl.ds(pl.multiple_of(high * hr, hr), hr)
+            cp = pltpu.make_async_copy(
+                l_hbm.at[pl.ds(c * tc, tc), :, my_rows], gath[c].at[i, 0], lsem.at[c]
+            )
+        else:
+            cp = pltpu.make_async_copy(l_hbm.at[pl.ds(c * tc, tc)], gath[c].at[i], lsem.at[c])
         cp.start()
         own_loads.append(cp)
 
@@ -63,7 +77,7 @@
 
     def piece(c, origin, to_right, own):
         dst = gath[c].at[origin]
-        src = l_hbm.at[pl.ds(c * tc, tc)] if own else dst
+        src = l_hbm.at[pl.ds(c * tc, tc)] if own and c != last else dst
         return pltpu.make_async_remote_copy(
             src_ref=src, dst_ref=dst,
             send_sem=(send_r if to_right else send_l).at[c, origin],
@@ -71,14 +85,35 @@
             device_id=right if to_right else left, device_id_type=MESH,
         )
 
-    for c in range(nch):
+    def send_own(c):
         @pl.when(has_r)
-        def _(c=c):
+        def _():
             piece(c, i, True, True).start()
 
         @pl.when(has_l)
-        def _(c=c):
+        def _():
             piece(c, i, False, True).start()
+
+    send_own(0)
+
+    def swap(k, src, dst):
+        return pltpu.make_async_remote_copy(
+            src_ref=src, dst_ref=dst, send_sem=xs.at[k], recv_sem=xr.at[k],
+            device_id=(g, i, across), device_id_type=MESH,
+        )
+
+    their_rows = pl.ds(pl.multiple_of((1 - high) * hr, hr), hr)
+    swap_l = swap(0, l_hbm.at[pl.ds(last * tc, tc), :, their_rows], gath[last].at[i, 1])
+    swap_c = swap(1, coeff_hbm, coeff_v)
+    swap_r = [
+        swap(2 + u * sd + r, r_hbm.at[last * tc + u, r], rcat_x.at[r, :, pl.ds(u * side, side)])
+        for u in range(tc) for r in range(sd)
+    ]
+    swaps = [swap_l, swap_c] + swap_r
+    for cp in swaps:
+        cp.start()
+    for c in range(1, last):
+        send_own(c)
 
     def relay(s, c):
         from_l, from_r = i - 1 - s, i + 1 + s
@@ -100,19 +135,24 @@
                 piece(c, from_r, False, False).start()
 
     wb_load.wait()
+    for cp in small_loads:
+        cp.wait()
     for cp in r_loads:
         cp.wait()
 
-    def wave_part(r, lo, hi):
+    def wave_part(r, lo, hi, theirs=False):
         def step(k, _):
-            for c in range(nch):
+            for c in (last,) if theirs else range(nch):
                 s0 = 2 * k
                 lhs = wb[r, pl.ds(s0, 2)].reshape(2 * side, side)
-                prod = jnp.dot(lhs, rcat[r, c], preferred_element_type=jnp.float32)
+                rhs = rcat_x[r] if theirs else rcat[r, c]
+                prod = jnp.dot(lhs, rhs, preferred_element_type=jnp.float32)
                 for j in range(2):
                     for u in range(tc):
-                        scaled = prod[j * side:(j + 1) * side, u * side:(u + 1) * side] * coeff[c * tc + u, s0 + j]
-                        wave[c][r * phys + s0 + j, u * side:(u + 1) * side, :] = scaled.astype(jnp.bfloat16)
+                        scale = (coeff_x if theirs else coeff)[c * tc + u, s0 + j]
+                        scaled = prod[j * side:(j + 1) * side, u * side:(u + 1) * side] * scale
+                        at = (u + (tc if theirs else 0)) * side
+                        wave[c][r * phys + s0 + j, at:at + side, :] = scaled.astype(jnp.bfloat16)
             return 0
 
         lax.fori_loop(lo, hi, step, 0)
@@ -120,29 +160,42 @@
     def product(c, q):
         r, s = q // phys, lax.rem(q, phys)
         own, sub = owner_ref[i * sd + r, s], sub_ref[i * sd + r, s]
-        lhs = jnp.concatenate([gath[c][own, u, sub] for u in range(tc)], axis=1)
+        if c == last:
+            parts = [gath[c][own, h, u, sub] for h in range(2) for u in range(tc)]
+        else:
+            parts = [gath[c][own, u, sub] for u in range(tc)]
+        lhs = jnp.concatenate(parts, axis=1)
         return jnp.dot(lhs, wave[c][q], preferred_element_type=jnp.float32)
 
     pairs = phys // 2
     wave_part(0, 0, pairs)
-    wave_part(1, 0, pairs // 2)
-    for r in range(2, sd):
+    if n > 2:
+        relay(0, 0)
+    for r in range(1, sd):
         wave_part(r, 0, pairs)
     if n > 2:
-        relay(0, 0)
-    wave_part(1, pairs // 2, pairs)
-    if n > 2:
-        for c in range(1, nch):
+        for c in range(1, last):
             relay(0, c)
-        def steps(s, _):
-            for c in range(nch):
-                relay(s, c)
-            return 0
+    for cp in swaps:
+        cp.wait_recv()
+    to_scalar = pltpu.make_async_copy(coeff_v, coeff_x, small_sem.at[3])
+    to_scalar.start()
+    to_scalar.wait()
+    for r in range(sd):
+        wave_part(r, 0, pairs, True)
+
+    def steps(s, _):
+        for c in range(last):
+            relay(s, c)
+        return 0
+
+    if n > 3:
         lax.fori_loop(1, n - 2, steps, 0)
     for cp in own_loads:
         cp.wait()
-
-    for c in range(nch - 1):
+    send_own(last)
+
+    for c in range(last - 1):
         relay(n - 2, c)
 
         def add(q, _, c=c):
@@ -151,8 +204,7 @@
             return 0
 
         lax.fori_loop(0, q_all, add, 0, unroll=2)
-    last = nch - 1
-    relay(n - 2, last)
+    relay(n - 2, last - 1)
 
     def hop1(k):
         return pltpu.make_async_remote_copy(
@@ -164,6 +216,12 @@
         return pltpu.make_async_remote_copy(
             src_ref=s2.at[k], dst_ref=r2.at[k], send_sem=ssem2.at[k], recv_sem=rsem2.at[k],
             device_id=(g, i, across), device_id_type=MESH,
+        )
+
+    def hop3(k):
+        return pltpu.make_async_remote_copy(
+            src_ref=s3.at[k], dst_ref=r3.at[k], send_sem=ssem3.at[k], recv_sem=rsem3.at[k],
+            device_id=(g, i, pair), device_id_type=MESH,
         )
 
     def rows_of(dest):
@@ -184,7 +242,8 @@
     for k in range(GROUPS):
         def finish(j, _, k=k):
             q = k * qg + j
-            acc[q] = acc[q] + product(last, q)
+            p = product(last - 1, q)
+            acc[q] = p if last == 1 else acc[q] + p
             for h in range(half):
                 s1[k, j, h] = acc[q, rows_of(2 * h + 1 - low)].astype(jnp.bfloat16)
             return 0
@@ -194,13 +253,30 @@
         if k >= 1:
             middle(k - 1)
     middle(GROUPS - 1)
+
+    def tail_steps(s, _):
+        relay(s, last)
+        return 0
+
+    lax.fori_loop(0, n - 1, tail_steps, 0)
+    for k in range(GROUPS):
+        def tail(j, _, k=k):
+            q = k * qg + j
+            bacc[q] = product(last, q)
+            s3[k, j] = bacc[q, rows_of(1 - low)].astype(jnp.bfloat16)
+            return 0
+
+        lax.fori_loop(0, qg, tail, 0, unroll=2)
+        hop3(k).start()
     for k in range(GROUPS):
         hop2(k).wait_recv()
+        hop3(k).wait_recv()
 
         def close(j, _, k=k):
             q = k * qg + j
             mine = acc[q, rows_of(t)] + r1[k, j, high].astype(jnp.float32)
             total = mine + r2[k, j].astype(jnp.float32)
+            total = total + bacc[q, rows_of(low)] + r3[k, j].astype(jnp.float32)
             out_ref[q // phys, lax.rem(q, phys)] = total.astype(jnp.bfloat16)
             return 0
 
@@ -209,6 +285,9 @@
     for k in range(GROUPS):
         hop1(k).wait_send()
         hop2(k).wait_send()
+        hop3(k).wait_send()
+    for cp in swaps:
+        cp.wait_send()
 
     def drain(o, _):
         for c in range(nch):
@@ -231,28 +310,38 @@
     nch = nt // tc
     rows, half, qg = side // nterm, nterm // 2, sd * phys // GROUPS
     bf, dma = jnp.bfloat16, pltpu.SemaphoreType.DMA
-    anywhere, smem = pl.BlockSpec(memory_space=pl.ANY), pl.BlockSpec(memory_space=pltpu.SMEM)
+    hbm = pl.BlockSpec(memory_space=pltpu.HBM)
     flops = 4 * nt * sd * phys * side ** 3
     return pl.pallas_call(
         functools.partial(body, n, nt, tc, sd, phys, side, nterm),
         out_shape=jax.ShapeDtypeStruct((sd, phys, rows, side), bf),
-        in_specs=[anywhere] * 3 + [smem] * 3,
+        in_specs=[hbm] * 6,
         out_specs=pl.BlockSpec(memory_space=pltpu.VMEM),
         scratch_shapes=[
+            pltpu.SMEM(site_coeff.shape, jnp.float32),
+            pltpu.SMEM(sub_sector.shape, jnp.int32),
+            pltpu.SMEM(sub_sector.shape, jnp.int32),
+            pltpu.SMEM(site_coeff.shape, jnp.float32),
+            pltpu.VMEM(site_coeff.shape, jnp.float32),
+            dma((4,)),
             pltpu.VMEM((sd, phys, side, side), bf),
             pltpu.VMEM((sd, nch, side, tc * side), bf),
+            pltpu.VMEM((sd, side, tc * side), bf),
             pltpu.VMEM((sd * phys, side, side), jnp.float32),
+            pltpu.VMEM((sd * phys, side // 2, side), jnp.float32),
             pltpu.VMEM((GROUPS, qg, half, rows, side), bf),
             pltpu.VMEM((GROUPS, qg, half, rows, side), bf),
-            pltpu.VMEM((GROUPS, qg, rows, side), bf),
-            pltpu.VMEM((GROUPS, qg, rows, side), bf),
         ]
-        + [pltpu.VMEM((n, tc, sd, side, side), bf)] * nch
-        + [pltpu.VMEM((sd * phys, tc * side, side), bf)] * nch
+        + [pltpu.VMEM((GROUPS, qg, rows, side), bf)] * 4
+        + [pltpu.VMEM((n, tc, sd, side, side), bf)] * (nch - 1)
+        + [pltpu.VMEM((n, 2, tc, sd, side // 2, side), bf)]
+        + [pltpu.VMEM((sd * phys, tc * side, side), bf)] * (nch - 1)
+        + [pltpu.VMEM((sd * phys, 2 * tc * side, side), bf)]
         + [dma, dma((nch,)), dma((nt, sd)), dma((nch, n)), dma((nch, n)), dma((nch, n))]
-        + [dma((GROUPS,))] * 4,
+        + [dma((GROUPS,))] * 6
+        + [dma((2 + tc * sd,))] * 2,
         compiler_params=pltpu.CompilerParams(
-            collective_id=0, has_side_effects=True, vmem_limit_bytes=52 << 20
+            collective_id=0, has_side_effects=True, vmem_limit_bytes=63 << 20
         ),
         cost_estimate=pl.CostEstimate(flops=flops, bytes_accessed=4 << 20, transcendentals=0),
         name="sigma",

time: 48.7 us -> 39.8 us (0.82)
  Pallas kernels: 43.7 us -> 38 us
  local copies, waits for them, and re-layouts: 4.75 us -> 1.67 us
    pallas_call x1, Pallas kernels: 43.7 us -> 38 us  [local(): pl.pallas_call(functools.partial(body, n, nt, tc, sd, phys, side, nterm),...]
    unnamed x11 -> x1, local copies, waits for them, and re-layouts: 4.75 us -> 1.67 us
where the time goes in v2:
time: 39.8 us; the launch traced here: 39.7 us
  Pallas kernels  38 us (95%)
  local copies, waits for them, and re-layouts  1.67 us (4%)
    pallas_call x1, Pallas kernels, local(): pl.pallas_call(functools.partial(body, n, nt, tc, sd, phys, side, nterm),...  38 us
    unnamed x1, local copies, waits for them, and re-layouts  1.67 us

profile of v2, /device:TPU:0, one launch (start us, length us, event | category | flops | bytes accessed | tf_op | source)
XLA Modules:
  0.0 39.7 jit_solution(4940688241531467700)
XLA Ops:
  0.0 38.0 %sigma.1 = bf16[2,16,32,128]{3,2,1,0:T(8,128)(2,1)} custom-call(bf16[2,16,128,128]{3,2,1,0:T(8,128)(2,1)} %wb_hbm.1, bf16[6,2,128,128]{3,2,1,0:T(8,128)(2,1)} %r_hbm.1, bf16[6,2,128,128]{3,2,1,0:T(8,128)(2,1)} %l_hbm.1, f32[6,16]{1,0:T(8,128)} %coeff_hbm.1, s32[8,16]{1,0:T(8,128)} %bitcast.1, s32[8,16]{1,0:T(8,128)} %sub_hbm.1), custom_call_target="tpu_custom_call" | custom-call | flops 1610612736 | bytes 4194304 | tf_op jit(solution)/shard_map/sigma/pallas_call | solution.py:315
  38.0 1.7 %copy.8 = bf16[2,16,32,128]{3,2,1,0:T(8,128)(2,1)} copy(bf16[2,16,32,128]{3,2,1,0:T(8,128)(2,1)} %sigma.1) | data formatting | bytes 524288

commit v3 on v2

--- a/solution.py
+++ b/solution.py
@@ -203,7 +203,7 @@
             acc[q] = p if c == 0 else acc[q] + p
             return 0
 
-        lax.fori_loop(0, q_all, add, 0, unroll=2)
+        lax.fori_loop(0, q_all, add, 0, unroll=4)
     relay(n - 2, last - 1)
 
     def hop1(k):
@@ -248,7 +248,7 @@
                 s1[k, j, h] = acc[q, rows_of(2 * h + 1 - low)].astype(jnp.bfloat16)
             return 0
 
-        lax.fori_loop(0, qg, finish, 0, unroll=2)
+        lax.fori_loop(0, qg, finish, 0, unroll=4)
         hop1(k).start()
         if k >= 1:
             middle(k - 1)
@@ -266,7 +266,7 @@
             s3[k, j] = bacc[q, rows_of(1 - low)].astype(jnp.bfloat16)
             return 0
 
-        lax.fori_loop(0, qg, tail, 0, unroll=2)
+        lax.fori_loop(0, qg, tail, 0, unroll=8)
         hop3(k).start()
     for k in range(GROUPS):
         hop2(k).wait_recv()
@@ -280,7 +280,7 @@
             out_ref[q // phys, lax.rem(q, phys)] = total.astype(jnp.bfloat16)
             return 0
 
-        lax.fori_loop(0, qg, close, 0, unroll=4)
+        lax.fori_loop(0, qg, close, 0, unroll=8)
 
     for k in range(GROUPS):
         hop1(k).wait_send()

time: 39.8 us -> 36.5 us (0.917)
  Pallas kernels: 38 us -> 34.7 us
    pallas_call x1, Pallas kernels: 38 us -> 34.7 us  [local(): pl.pallas_call(functools.partial(body, n, nt, tc, sd, phys, side, nterm),...]
where the time goes in v3:
time: 36.5 us; the launch traced here: 36.3 us
  Pallas kernels  34.7 us (95%)
  local copies, waits for them, and re-layouts  1.67 us (5%)
    pallas_call x1, Pallas kernels, local(): pl.pallas_call(functools.partial(body, n, nt, tc, sd, phys, side, nterm),...  34.7 us
    unnamed x1, local copies, waits for them, and re-layouts  1.67 us

profile of v3, /device:TPU:0, one launch (start us, length us, event | category | flops | bytes accessed | tf_op | source)
XLA Modules:
  0.0 36.3 jit_solution(12975436493947525550)
XLA Ops:
  0.0 34.7 %sigma.1 = bf16[2,16,32,128]{3,2,1,0:T(8,128)(2,1)} custom-call(bf16[2,16,128,128]{3,2,1,0:T(8,128)(2,1)} %wb_hbm.1, bf16[6,2,128,128]{3,2,1,0:T(8,128)(2,1)} %r_hbm.1, bf16[6,2,128,128]{3,2,1,0:T(8,128)(2,1)} %l_hbm.1, f32[6,16]{1,0:T(8,128)} %coeff_hbm.1, s32[8,16]{1,0:T(8,128)} %bitcast.1, s32[8,16]{1,0:T(8,128)} %sub_hbm.1), custom_call_target="tpu_custom_call" | custom-call | flops 1610612736 | bytes 4194304 | tf_op jit(solution)/shard_map/sigma/pallas_call | solution.py:315
  34.7 1.7 %copy.8 = bf16[2,16,32,128]{3,2,1,0:T(8,128)(2,1)} copy(bf16[2,16,32,128]{3,2,1,0:T(8,128)(2,1)} %sigma.1) | data formatting | bytes 524288

commit v4 on v3

--- a/solution.py
+++ b/solution.py
@@ -205,6 +205,11 @@
 
         lax.fori_loop(0, q_all, add, 0, unroll=4)
     relay(n - 2, last - 1)
+    inner = jnp.logical_and(has_r, has_l)
+
+    @pl.when(inner)
+    def _():
+        relay(0, last)
 
     def hop1(k):
         return pltpu.make_async_remote_copy(
@@ -255,7 +260,10 @@
     middle(GROUPS - 1)
 
     def tail_steps(s, _):
-        relay(s, last)
+        @pl.when(jnp.logical_not(jnp.logical_and(inner, s == 0)))
+        def _():
+            relay(s, last)
+
         return 0
 
     lax.fori_loop(0, n - 1, tail_steps, 0)

time: 36.5 us -> 37.1 us (1.016)
  Pallas kernels: 34.7 us -> 35.3 us
    pallas_call x1, Pallas kernels: 34.7 us -> 35.3 us  [local(): pl.pallas_call(functools.partial(body, n, nt, tc, sd, phys, side, nterm),...]
where the time goes in v4:
time: 37.1 us; the launch traced here: 37 us
  Pallas kernels  35.3 us (95%)
  local copies, waits for them, and re-layouts  1.67 us (5%)
    pallas_call x1, Pallas kernels, local(): pl.pallas_call(functools.partial(body, n, nt, tc, sd, phys, side, nterm),...  35.3 us
    unnamed x1, local copies, waits for them, and re-layouts  1.67 us

profile of v4, /device:TPU:0, one launch (start us, length us, event | category | flops | bytes accessed | tf_op | source)
XLA Modules:
  0.0 37.0 jit_solution(17520153369577789012)
XLA Ops:
  0.0 35.3 %sigma.1 = bf16[2,16,32,128]{3,2,1,0:T(8,128)(2,1)} custom-call(bf16[2,16,128,128]{3,2,1,0:T(8,128)(2,1)} %wb_hbm.1, bf16[6,2,128,128]{3,2,1,0:T(8,128)(2,1)} %r_hbm.1, bf16[6,2,128,128]{3,2,1,0:T(8,128)(2,1)} %l_hbm.1, f32[6,16]{1,0:T(8,128)} %coeff_hbm.1, s32[8,16]{1,0:T(8,128)} %bitcast.1, s32[8,16]{1,0:T(8,128)} %sub_hbm.1), custom_call_target="tpu_custom_call" | custom-call | flops 1610612736 | bytes 4194304 | tf_op jit(solution)/shard_map/sigma/pallas_call | solution.py:323
  35.3 1.7 %copy.8 = bf16[2,16,32,128]{3,2,1,0:T(8,128)(2,1)} copy(bf16[2,16,32,128]{3,2,1,0:T(8,128)(2,1)} %sigma.1) | data formatting | bytes 524288
